TPU v7x, 32 devices: a whole 2x2x4 slice. The times are simulated.
32 devices in a mesh: sens: 8 (over z, y), unk: 4 (over x, core).
Axes of the slice: x: 2, y: 2, z: 4, core: 2. Of those that a mesh axis runs over, the one named last changes fastest.
Arguments:
- signals: float32 [256, 4, 256], P('sens', None, 'unk'), may hold values from -6 to 6
- kernel: float32 [256, 32, 4096], P('sens', None, 'unk'), may hold values from -0.046875 to 0.046875
- tap_weights: float32 [17, 4096], P(None, 'unk'), may hold values from -1.5 to 1.5
Outputs:
- hessian_action: float32 [256, 4, 256], P('sens', None, 'unk')
All inputs are finite; a program needn't handle non-finite values.
Results may differ from a plain program's by a relative error of at most 0.00008.
Values sent between devices are 32-bit elements; how exact they have to be, the bound alone decides.
A program may use at most 64 MiB of HBM per device.

v0:
```python
import jax
import jax.numpy as jnp
from jax import lax
from jax.sharding import PartitionSpec as P


def hankel(signals, lag_count):
    steps_count = signals.shape[2]
    padded = jnp.pad(signals, ((0, 0), (0, 0), (0, lag_count)))
    return jnp.stack(
        [padded[:, :, offset : offset + steps_count] for offset in range(lag_count)], axis=1
    )


def skew_sum(product):
    sens_rows, vectors, lag_count, steps_count = product.shape
    padded = jnp.pad(product, ((0, 0), (0, 0), (0, 0), (0, lag_count)))
    flattened = padded.reshape(sens_rows, vectors, lag_count * (steps_count + lag_count))
    flattened = flattened[:, :, : lag_count * (steps_count + lag_count - 1)]
    sheared = flattened.reshape(sens_rows, vectors, lag_count, steps_count + lag_count - 1)
    return jnp.sum(sheared[..., :steps_count], axis=2)


def filter_padded(padded, tap_weights, steps_count):
    result = jnp.zeros((padded.shape[0], padded.shape[1], steps_count), jnp.float32)
    for tap_index in range(tap_weights.shape[0]):
        result = (
            result
            + tap_weights[tap_index][:, None, None]
            * padded[:, :, tap_index : tap_index + steps_count]
        )
    return result


def smooth_time(series, tap_weights, half_width):
    padded = jnp.pad(series, ((0, 0), (0, 0), (half_width, half_width)))
    return filter_padded(padded, tap_weights, series.shape[2])


def on_device(signals, kernel, tap_weights):
    whole_signals = lax.all_gather(signals, "unk", axis=2, tiled=True)
    sens_rows, lag_count, unk_dev = kernel.shape
    half_width = (tap_weights.shape[0] - 1) // 2
    window = hankel(whole_signals, lag_count)
    row_count = unk_dev // lax.axis_size("sens")
    kernel_part = kernel
    own_rows = lax.psum_scatter(
        jnp.einsum("slu,slbt->ubt", kernel_part, window, precision=lax.Precision.HIGHEST),
        "sens",
        scatter_dimension=0,
        tiled=True,
    )
    local_taps = lax.dynamic_slice_in_dim(
        tap_weights, lax.axis_index("sens") * row_count, row_count, 1
    )
    smoothed = smooth_time(own_rows, local_taps, half_width)
    kernel_part = kernel
    product = jnp.einsum(
        "slu,ubt->sblt",
        kernel_part,
        lax.all_gather(smoothed, "sens", axis=0, tiled=True),
        precision=lax.Precision.HIGHEST,
    )
    partial_value = skew_sum(product)
    return lax.psum_scatter(partial_value, "unk", scatter_dimension=2, tiled=True)


def solution(mesh):
    return jax.shard_map(
        on_device,
        mesh=mesh,
        in_specs=(P("sens", None, "unk"), P("sens", None, "unk"), P(None, "unk")),
        out_specs=P("sens", None, "unk"),
        check_vma=False,
    )
```

profile of v0, /device:TPU:1, one launch (start us, length us, event | category | flops | bytes accessed | tf_op | source)
XLA Modules:
  0.0 283.2 jit_solution(8565602880728184570)
XLA Ops:
  6.5 0.9 copy.38
  7.5 8.5 %all_gather.6 = f32[32,4,256]{0,1,2:T(4,128)S(1)} all-gather(f32[32,4,64]{0,1,2:T(4,128)S(1)} %copy.38), channel_id=1, replica_groups=mesh['sens'=8,'unk'=4] {'unk'}, dimensions={2}, use_global_device_ids=true | all-gather | bytes 163840 | tf_op jit(solution)/shard_map/all_gather | solution.py:41
  16.0 0.2 copy.39
  16.4 0.1 fusion.32
  16.5 0.1 fusion.34
  16.9 0.1 fusion.42
  17.0 0.1 fusion.44
  17.4 0.1 fusion.50
  19.4 15.8 %fusion.6 = f32[1024,4,256]{0,2,1:T(8,128)} fusion(f32[32,32,4,256]{3,0,1,2:T(8,128)S(1)} %fusion.88, f32[32,32,1024]{2,1,0:T(8,128)S(1)} %copy-done), kind=kOutput, calls=%fused_computation.7 | convolution fusion | flops 12884901888 | bytes 12582912 | tf_op jit(solution)/shard_map/slu,slbt->ubt/dot_general | solution.py:48
  35.3 1.1 dynamic-slice_bitcast_fusion.16
  36.4 87.8 %reduce-scatter.5.cloned.1.call-done = f32[128,4,256]{0,2,1:T(8,128)} async-done(((f32[1024,4,256]{0,2,1:T(8,128)}), f32[128,4,256]{0,2,1:T(8,128)}) %reduce-scatter.5.cloned.1.call-update) | async-done | bytes 524304 | tf_op jit(solution)/shard_map/reduce_scatter | solution.py:47
  124.3 7.5 %multiply_add_fusion = f32[128,4,256]{0,2,1:T(8,128)} fusion(f32[128,4,256]{0,2,1:T(8,128)} %reduce-scatter.5.cloned.1.call-done, f32[128]{0:T(128)S(1)} %get-tuple-element.21, f32[128]{0:T(128)S(1)} %get-tuple-element.6, f32[128]{0:T(128)S(1)} %get-tuple-element.7, f32[128]{0:T(128)S(1)} %get-tuple-element.8, f32[128]{0:T(128)S(1)} %get-tuple-element.9, ...), kind=kLoop, calls=%fused_computation.40 | loop fusion | flops 4325376 | bytes 1057280 | tf_op jit(solution)/shard_map/add | solution.py:28
  131.8 0.2 reduce-scatter.7.cloned.1.call-start
  132.0 74.2 %all-gather.2.cloned.1.call-done = f32[1024,4,256]{0,2,1:T(8,128)} async-done(((f32[128,4,256]{0,2,1:T(8,128)}), f32[1024,4,256]{0,2,1:T(8,128)}) %all-gather.2.cloned.1.call-update) | async-done | bytes 4194320 | tf_op jit(solution)/shard_map/all_gather | solution.py:61
  206.2 17.3 %fusion.9 = f32[32,4,32,256]{3,2,0,1:T(8,128)S(1)} fusion(f32[32,32,1024]{2,1,0:T(8,128)} %param.4, f32[1024,4,256]{0,2,1:T(8,128)} %all-gather.2.cloned.1.call-done), kind=kOutput, calls=%fused_computation.8 | convolution fusion | flops 12884901888 | bytes 12582912 | tf_op jit(solution)/shard_map/slu,ubt->sblt/dot_general | solution.py:58
  223.5 3.4 %pad.14 = f32[32,4,32,288]{3,2,0,1:T(8,128)} pad(f32[32,4,32,256]{3,2,0,1:T(8,128)S(1)} %fusion.9, f32[]{:T(128)} %constant.14.clone.1), padding=0_0x0_0x0_0x0_32 | pad | bytes 8912900 | tf_op jit(solution)/shard_map/jit(_pad)/pad | solution.py:17
  226.9 6.9 %reshape.23 = f32[32,4,9216]{2,0,1:T(8,128)} reshape(f32[32,4,32,288]{3,2,0,1:T(8,128)} %pad.14) | data formatting | bytes 9437184 | tf_op jit(solution)/shard_map/reshape | solution.py:18
  233.8 9.1 %reshape.24 = f32[32,4,32,287]{3,2,0,1:T(8,128)} reshape(f32[32,4,9184]{2,0,1:T(8,128)} %bitcast.254) | data formatting | bytes 9404416 | tf_op jit(solution)/shard_map/reshape | solution.py:20
  243.0 2.9 %slice_reduce_fusion = f32[32,4,256]{2,0,1:T(8,128)S(1)} fusion(f32[32,4,32,287]{3,2,0,1:T(8,128)} %reshape.24), kind=kLoop, calls=%fused_computation | loop fusion | flops 1015808 | bytes 4325376 | tf_op jit(solution)/shard_map/reduce_sum | solution.py:21
  245.8 4.4 %copy.78 = f32[32,4,256]{1,0,2:T(8,128)} copy(f32[32,4,256]{2,0,1:T(8,128)S(1)} %slice_reduce_fusion) | data formatting | bytes 262144
  250.3 5.5 %reshape.29 = f32[256,128]{1,0:T(8,128)} reshape(f32[256,32,4]{2,1,0:T(8,128)} %bitcast.255) | data formatting | bytes 262144
  255.8 17.9 %reduce-scatter.7.cloned.1.call-done = f32[64,128]{1,0:T(8,128)} async-done(((f32[256,128]{1,0:T(8,128)}), f32[64,128]{1,0:T(8,128)}) %reduce-scatter.7.cloned.1.call-update) | async-done | bytes 32784
  273.6 1.8 reshape.30
  275.5 1.2 copy.79
  (34 shorter events, 2.6 us)
Async XLA Ops:
  6.5 117.7 %reduce-scatter.5.cloned.1.call-start = ((), (), s32[]{:S(2)}) async-start(), calls=%async_computation.2 | async-start | bytes 4718592 | tf_op jit(solution)/shard_map/reduce_scatter | solution.py:47
  16.2 3.2 %copy-start = (f32[32,32,1024]{2,1,0:T(8,128)S(1)}, f32[32,32,1024]{2,1,0:T(8,128)}, u32[]{:S(2)}) copy-start(f32[32,32,1024]{2,1,0:T(8,128)} %param.4) | copy-start | bytes 12582916
  35.2 171.0 %all-gather.2.cloned.1.call-start = ((), (), s32[]{:S(2)}) async-start(), calls=%async_computation.3 | async-start | bytes 4718592 | tf_op jit(solution)/shard_map/all_gather | solution.py:61
  131.8 141.9 %reduce-scatter.7.cloned.1.call-start = ((), (), s32[]{:S(2)}) async-start(), calls=%async_computation.4 | async-start | bytes 163840
Sparse Core Ops, SparseCore 0:
  35.4 88.8 reduce-scatter.4
  131.9 74.2 all-gather.1
  255.9 17.7 reduce-scatter.6
where the time goes:
time: 285 us; the launch traced here: 283 us
  waiting for transfers between devices  180 us (63%)
  local copies, waits for them, and re-layouts  37.7 us (13%)
  matrix products  33 us (12%)
  between operations  13.4 us (5%)
  other arithmetic  10.3 us (4%)
  blocking collectives  8.51 us (3%)
    reduce_scatter x1, waiting for transfers between devices, on_device(): lax.psum_scatter(jnp.einsum('slu,slbt->ubt', kernel_part, window, precisi...  87.8 us
    all_gather x1, waiting for transfers between devices, on_device(): lax.all_gather(smoothed, 'sens', axis=0, tiled=True)  74.2 us
    unnamed x4, waiting for transfers between devices  17.9 us
    dot_general x1, matrix products, on_device(): jnp.einsum('slu,ubt->sblt', kernel_part, lax.all_gather(smoothed, 'sens',...  17.3 us
    unnamed x38, local copies, waits for them, and re-layouts  16.8 us
    dot_general x1, matrix products, on_device(): jnp.einsum('slu,slbt->ubt', kernel_part, window, precision=lax.Precision....  15.8 us
    reshape x1, local copies, waits for them, and re-layouts, skew_sum(): flattened.reshape(sens_rows, vectors, lag_count, steps_count + lag_count...  9.13 us
    all_gather x1, blocking collectives, on_device(): whole_signals = lax.all_gather(signals, 'unk', axis=2, tiled=True)  8.51 us
  transfers between devices with their start and end apart: 3, of which 3 were waited for; matrix products, arithmetic and copies ran while one was open for 0% of the time, Pallas kernels for 0%

commit v1 on v0

v1 whole, which is shorter than its diff:
```python
import functools

import jax
import jax.numpy as jnp
from jax import lax
from jax.experimental import pallas as pl
from jax.experimental.pallas import tpu as pltpu
from jax.sharding import PartitionSpec as P

MESH = pl.DeviceIdType.MESH
VMEM_LIMIT = 56 * 1024 * 1024
HOP = 2


def hankel(signals, lag_count):
    steps_count = signals.shape[2]
    padded = jnp.pad(signals, ((0, 0), (0, 0), (0, lag_count)))
    return jnp.stack(
        [padded[:, :, offset : offset + steps_count] for offset in range(lag_count)], axis=1
    )


def greet(axis, peers):
    barrier = pltpu.get_barrier_semaphore()
    for peer in peers:
        pl.semaphore_signal(barrier, inc=1, device_id={axis: peer}, device_id_type=MESH)
    pl.semaphore_wait(barrier, len(peers))


def split(x):
    high = x.astype(jnp.bfloat16)
    return high, (x - high.astype(jnp.float32)).astype(jnp.bfloat16)


def smooth_rows(x, taps, steps_count):
    tap_count = taps.shape[1]
    half = (tap_count - 1) // 2
    pieces = []
    for first in range(0, x.shape[1], steps_count):
        part = x[:, first : first + steps_count]
        time = lax.broadcasted_iota(jnp.int32, part.shape, 1)
        total = taps[:, half : half + 1] * part
        for tap in range(tap_count):
            offset = tap - half
            if offset == 0:
                continue
            moved = pltpu.roll(part, (-offset) % steps_count, 1)
            inside = (time < steps_count - offset) if offset > 0 else (time >= -offset)
            total = total + taps[:, tap : tap + 1] * jnp.where(inside, moved, 0.0)
        pieces.append(total)
    return jnp.concatenate(pieces, axis=1)


def sum_kernel(chain, chunks, steps_count, p_ref, tap_ref, out_ref, y_in, own, up_in, up_out,
               down_in, down_out, sems):
    n = 2 * chain
    me = lax.axis_index("sens")
    z, y = me // 2, me % 2
    mate = z * 2 + (1 - y)
    above, below = jnp.minimum(me + 2, n - 1), jnp.maximum(me - 2, 0)
    half_rows = p_ref.shape[0] // 2
    rows = half_rows // chunks
    not_last, not_first = z < chain - 1, z > 0

    def chunk(c):
        return pl.ds(pl.multiple_of(c * rows, rows), rows)

    def half_chunk(h, c):
        return pl.ds(pl.multiple_of(h * half_rows + c * rows, rows), rows)

    def y_copy(c):
        return pltpu.make_async_remote_copy(
            src_ref=p_ref.at[half_chunk(1 - y, c)], dst_ref=y_in.at[chunk(c)],
            send_sem=sems.at[0, c], recv_sem=sems.at[1, c],
            device_id={"sens": mate}, device_id_type=MESH)

    def up_copy(c):
        return pltpu.make_async_remote_copy(
            src_ref=up_out.at[chunk(c)], dst_ref=up_in.at[chunk(c)],
            send_sem=sems.at[2, c], recv_sem=sems.at[3, c],
            device_id={"sens": above}, device_id_type=MESH)

    def down_copy(c):
        return pltpu.make_async_remote_copy(
            src_ref=down_out.at[chunk(c)], dst_ref=down_in.at[chunk(c)],
            send_sem=sems.at[4, c], recv_sem=sems.at[5, c],
            device_id={"sens": below}, device_id_type=MESH)

    def back_copy(c):
        part = out_ref.at[half_chunk(y, c)]
        return pltpu.make_async_remote_copy(
            src_ref=part, dst_ref=part,
            send_sem=sems.at[6, c], recv_sem=sems.at[7, c],
            device_id={"sens": mate}, device_id_type=MESH)

    def back_wait(c):
        part = out_ref.at[half_chunk(1 - y, c)]
        pltpu.make_async_remote_copy(
            src_ref=part, dst_ref=part,
            send_sem=sems.at[6, c], recv_sem=sems.at[7, c],
            device_id={"sens": mate}, device_id_type=MESH).wait_recv()

    barrier = pltpu.get_barrier_semaphore()
    pl.semaphore_signal(barrier, inc=1, device_id={"sens": mate}, device_id_type=MESH)

    @pl.when(not_last)
    def _():
        pl.semaphore_signal(barrier, inc=1, device_id={"sens": above}, device_id_type=MESH)

    @pl.when(not_first)
    def _():
        pl.semaphore_signal(barrier, inc=1, device_id={"sens": below}, device_id_type=MESH)

    pl.semaphore_wait(barrier, 1 + jnp.where(not_last, 1, 0) + jnp.where(not_first, 1, 0))

    @pl.loop(0, chunks)
    def _(c):
        y_copy(c).start()

    lag_up, lag_down = HOP * z, HOP * (chain - 1 - z)
    lag_last = HOP * (chain - 1)

    @pl.loop(0, chunks + lag_last)
    def _(step):
        @pl.when(step < chunks)
        def _():
            y_copy(step).wait_recv()
            own[chunk(step)] = p_ref[half_chunk(y, step)] + y_in[chunk(step)]

        up = step - lag_up

        @pl.when((up >= 0) & (up < chunks))
        def _():
            @pl.when(not_first)
            def _():
                up_copy(up).wait_recv()

            @pl.when(jnp.logical_not(not_first))
            def _():
                up_in[chunk(up)] = jnp.zeros((rows, p_ref.shape[1]), jnp.float32)

            @pl.when(not_last)
            def _():
                up_out[chunk(up)] = own[chunk(up)] + up_in[chunk(up)]
                up_copy(up).start()

        down = step - lag_down

        @pl.when((down >= 0) & (down < chunks))
        def _():
            @pl.when(not_last)
            def _():
                down_copy(down).wait_recv()

            @pl.when(jnp.logical_not(not_last))
            def _():
                down_in[chunk(down)] = jnp.zeros((rows, p_ref.shape[1]), jnp.float32)

            @pl.when(not_first)
            def _():
                down_out[chunk(down)] = own[chunk(down)] + down_in[chunk(down)]
                down_copy(down).start()

        last = step - lag_last

        @pl.when((last >= 0) & (last < chunks))
        def _():
            total = own[chunk(last)] + up_in[chunk(last)] + down_in[chunk(last)]
            out_ref[half_chunk(y, last)] = smooth_rows(
                total, tap_ref[half_chunk(y, last)], steps_count
            )
            back_copy(last).start()

    @pl.loop(0, chunks)
    def _(c):
        y_copy(c).wait_send()
        back_copy(c).wait_send()
        back_wait(c)

        @pl.when(not_last)
        def _():
            up_copy(c).wait_send()

        @pl.when(not_first)
        def _():
            down_copy(c).wait_send()


def summed_smoothed(partial, taps, steps_count, sens_count):
    unk_dev, columns = partial.shape
    chunks = max(1, unk_dev // 2 // 32)
    half = pltpu.VMEM((unk_dev // 2, columns), jnp.float32)
    return pl.pallas_call(
        functools.partial(sum_kernel, sens_count // 2, chunks, steps_count),
        out_shape=jax.ShapeDtypeStruct(partial.shape, jnp.float32),
        in_specs=[pl.BlockSpec(memory_space=pltpu.VMEM)] * 2,
        out_specs=pl.BlockSpec(memory_space=pltpu.VMEM),
        scratch_shapes=[half] * 6 + [pltpu.SemaphoreType.DMA((8, chunks))],
        compiler_params=pltpu.CompilerParams(
            collective_id=0, has_side_effects=True, vmem_limit_bytes=VMEM_LIMIT
        ),
    )(partial, taps)


def forward_kernel(lag_count, vectors, k_ref, s_ref, out_ref, high, low):
    @pl.when(pl.program_id(0) == 0)
    def _():
        high[...], low[...] = split(s_ref[...])

    k_high, k_low = split(k_ref[...])
    dot = functools.partial(jnp.dot, preferred_element_type=jnp.float32)
    steps_count = s_ref.shape[1] // vectors
    time = lax.broadcasted_iota(jnp.int32, (lag_count, steps_count), 1)
    lag = lax.broadcasted_iota(jnp.int32, (lag_count, steps_count), 0)
    for vector in range(vectors):
        columns = slice(vector * steps_count, (vector + 1) * steps_count)
        product = dot(k_high, high[:, columns]) + (
            dot(k_high, low[:, columns]) + dot(k_low, high[:, columns])
        )
        for sensor in range(k_ref.shape[0] // lag_count):
            part = product[sensor * lag_count : (sensor + 1) * lag_count]
            sheared = pltpu.roll(part, 0, 1, stride=1, stride_axis=0)
            row = jnp.sum(jnp.where(time >= lag, sheared, 0.0), axis=0, keepdims=True)
            place = sensor * vectors + vector
            out_ref[place : place + 1, :] = row


def forward(kernel, smoothed, lag_count, vectors):
    rows, unk_dev = kernel.shape
    columns = smoothed.shape[1]
    group = min(8, rows // lag_count)
    sens_rows = rows // lag_count
    return pl.pallas_call(
        functools.partial(forward_kernel, lag_count, vectors),
        grid=(sens_rows // group,),
        out_shape=jax.ShapeDtypeStruct((sens_rows * vectors, columns // vectors), jnp.float32),
        in_specs=[
            pl.BlockSpec((group * lag_count, unk_dev), lambda i: (i, 0)),
            pl.BlockSpec((unk_dev, columns), lambda i: (0, 0)),
        ],
        out_specs=pl.BlockSpec((group * vectors, columns // vectors), lambda i: (i, 0)),
        scratch_shapes=[pltpu.VMEM((unk_dev, columns), jnp.bfloat16)] * 2,
        compiler_params=pltpu.CompilerParams(vmem_limit_bytes=VMEM_LIMIT),
    )(kernel, smoothed)


def scatter_kernel(n, x_ref, out_ref, stage, landed, send_sem, recv_sem):
    me = lax.axis_index("unk")
    width = out_ref.shape[1]
    greet("unk", [lax.rem(me + k, n) for k in range(1, n)])
    for piece in range(n):
        stage[piece] = x_ref[:, piece * width : (piece + 1) * width]

    def copy(k):
        peer = lax.rem(me + k, n)
        return pltpu.make_async_remote_copy(
            src_ref=stage.at[peer], dst_ref=landed.at[k],
            send_sem=send_sem.at[k], recv_sem=recv_sem.at[k],
            device_id={"unk": peer}, device_id_type=MESH)

    for k in range(1, n):
        copy(k).start()
    total = stage[me]
    for k in range(1, n):
        copy(k).wait_recv()
        total = total + landed[k]
    out_ref[...] = total
    for k in range(1, n):
        copy(k).wait_send()


def scattered(partial, n):
    rows, steps_count = partial.shape
    width = steps_count // n
    return pl.pallas_call(
        functools.partial(scatter_kernel, n),
        out_shape=jax.ShapeDtypeStruct((rows, width), jnp.float32),
        in_specs=[pl.BlockSpec(memory_space=pltpu.VMEM)],
        out_specs=pl.BlockSpec(memory_space=pltpu.VMEM),
        scratch_shapes=[
            pltpu.VMEM((n, rows, width), jnp.float32),
            pltpu.VMEM((n, rows, width), jnp.float32),
            pltpu.SemaphoreType.DMA((n,)),
            pltpu.SemaphoreType.DMA((n,)),
        ],
        compiler_params=pltpu.CompilerParams(
            collective_id=1, has_side_effects=True, vmem_limit_bytes=VMEM_LIMIT
        ),
    )(partial)


def on_device(signals, kernel, tap_weights, *, sens_count, unk_count):
    whole_signals = lax.all_gather(signals, "unk", axis=2, tiled=True)
    sens_rows, lag_count, unk_dev = kernel.shape
    _, vectors, steps_count = whole_signals.shape
    flat_kernel = kernel.reshape(sens_rows * lag_count, unk_dev)
    window = hankel(whole_signals, lag_count)
    window = window.reshape(sens_rows * lag_count, vectors * steps_count)
    partial = jnp.einsum("ku,kt->ut", flat_kernel, window, precision=lax.Precision.HIGH)
    smoothed = summed_smoothed(partial, tap_weights.T, steps_count, sens_count)
    product = forward(flat_kernel, smoothed, lag_count, vectors)
    return scattered(product, unk_count).reshape(signals.shape)


def solution(mesh):
    return jax.shard_map(
        functools.partial(
            on_device, sens_count=mesh.shape["sens"], unk_count=mesh.shape["unk"]
        ),
        mesh=mesh,
        in_specs=(P("sens", None, "unk"), P("sens", None, "unk"), P(None, "unk")),
        out_specs=P("sens", None, "unk"),
        check_vma=False,
    )
```

time: 285 us -> 188 us (0.66)
  waiting for transfers between devices: 180 us -> 0 us
  Pallas kernels: 0 us -> 118 us
  matrix products: 33 us -> 9.93 us
  between operations: 13.4 us -> 0.05 us
  local copies, waits for them, and re-layouts: 37.7 us -> 51 us
  other arithmetic: 10.3 us -> 0 us
    pallas_call x0 -> x3, Pallas kernels: none -> 118 us  [the longest x1 98.5 us: summed_smoothed(): pl.pallas_call(functools.partial(sum_kernel, sens_count // 2, chunks, ste...]
    reduce_scatter x1 -> x0, waiting for transfers between devices: 87.8 us -> none  [on_device(): lax.psum_scatter(jnp.einsum('slu,slbt->ubt', kernel_part, window, precisi...]
    all_gather x1 -> x0, waiting for transfers between devices: 74.2 us -> none  [on_device(): lax.all_gather(smoothed, 'sens', axis=0, tiled=True)]
    dot_general x2 -> x1, matrix products: 33 us -> 9.93 us  [on_device(): jnp.einsum('ku,kt->ut', flat_kernel, window, precision=lax.Precision.HIGH)]
    unnamed x38 -> x37, local copies, waits for them, and re-layouts: 16.8 us -> 35.1 us
    unnamed x4 -> x0, waiting for transfers between devices: 17.9 us -> none
    reshape x2 -> x0, local copies, waits for them, and re-layouts: 16.1 us -> none  [the longest x1 9.13 us: skew_sum(): flattened.reshape(sens_rows, vectors, lag_count, steps_count + lag_count...]
    another operation x1 -> x2, local copies, waits for them, and re-layouts: 0.1 us -> 15.9 us  [hankel(): jnp.stack([padded[:, :, offset:offset + steps_count] for offset in range(...]
  transfers between devices with their start and end apart: 3 -> 0, of which waited for: 3 -> 0; matrix products, arithmetic and copies ran while one was open for 0% -> 0% of each run, Pallas kernels for 0% -> 0%
where the time goes in v1:
time: 188 us
  Pallas kernels  118 us (63%)
  local copies, waits for them, and re-layouts  51 us (27%)
  matrix products  9.93 us (5%)
  blocking collectives  8.51 us (5%)
    pallas_call x1, Pallas kernels, summed_smoothed(): pl.pallas_call(functools.partial(sum_kernel, sens_count // 2, chunks, ste...  98.5 us
    unnamed x37, local copies, waits for them, and re-layouts  35.1 us
    another operation x2, local copies, waits for them, and re-layouts, hankel(): jnp.stack([padded[:, :, offset:offset + steps_count] for offset in range(...  15.9 us
    pallas_call x1, Pallas kernels, forward(): pl.pallas_call(functools.partial(forward_kernel, lag_count, vectors), gri...  11.7 us
    dot_general x1, matrix products, on_device(): jnp.einsum('ku,kt->ut', flat_kernel, window, precision=lax.Precision.HIGH)  9.93 us
    all_gather x1, blocking collectives, on_device(): whole_signals = lax.all_gather(signals, 'unk', axis=2, tiled=True)  8.51 us
    pallas_call x1, Pallas kernels, scattered(): pl.pallas_call(functools.partial(scatter_kernel, n), out_shape=jax.ShapeD...  7.83 us

profile of v1, /device:TPU:1, one launch (start us, length us, event | category | flops | bytes accessed | tf_op | source)
XLA Modules:
  0.0 187.5 jit_solution(8627830376209911392)
XLA Ops:
  0.0 0.9 copy.49
  0.9 8.5 %all_gather.3 = f32[32,4,256]{0,1,2:T(4,128)S(1)} all-gather(f32[32,4,64]{0,1,2:T(4,128)S(1)} %copy.49), channel_id=1, replica_groups=mesh['sens'=8,'unk'=4] {'unk'}, dimensions={2}, use_global_device_ids=true | all-gather | bytes 163840 | tf_op jit(solution)/shard_map/all_gather | solution.py:293
  10.3 0.9 bitcast_dynamic-update-slice_fusion.30
  11.2 0.9 bitcast_dynamic-update-slice_fusion.29
  15.8 0.9 bitcast_dynamic-update-slice_fusion.24
  17.6 0.9 bitcast_dynamic-update-slice_fusion.22
  21.3 0.9 bitcast_dynamic-update-slice_fusion.18
  23.1 0.9 bitcast_dynamic-update-slice_fusion.16
  24.0 1.0 bitcast_dynamic-update-slice_fusion.15
  25.0 1.0 bitcast_dynamic-update-slice_fusion.14
  27.8 0.9 bitcast_dynamic-update-slice_fusion.11
  30.5 0.9 bitcast_dynamic-update-slice_fusion.8
  31.4 0.9 bitcast_dynamic-update-slice_fusion.7
  32.4 0.9 bitcast_dynamic-update-slice_fusion.6
  35.1 0.9 bitcast_dynamic-update-slice_fusion.3
  36.0 0.9 bitcast_dynamic-update-slice_fusion.2
  38.8 15.0 %copy.50 = f32[32,32,4,256]{3,2,1,0:T(4,128)} copy(f32[32,32,4,256]{0,2,3,1:T(4,128)} %bitcast_dynamic-update-slice_fusion) | data formatting | bytes 8388608 | tf_op jit(solution)/shard_map/stack | solution.py:18
  53.8 3.2 %copy.54 = f32[128,8,4,256]{3,1,2,0:T(8,128)S(1)} copy(f32[128,8,4,256]{3,2,1,0:T(4,128)} %bitcast.74) | data formatting | bytes 8388608
  57.0 9.9 %convolution_bitcast_fusion.p_ref = f32[1024,1024]{1,0:T(8,128)} fusion(f32[1024,1024]{1,0:T(8,128)S(1)} %bitcast.77, f32[1024,1024]{1,0:T(8,128)} %bitcast.75), kind=kOutput, calls=%fused_computation | convolution fusion | flops 6442450944 | bytes 12582912 | tf_op jit(solution)/shard_map/ku,kt->ut/dot_general | solution.py:299
  67.0 1.1 copy.52
  68.0 98.5 %shard_map.37.s_ref = f32[1024,1024]{1,0:T(8,128)} custom-call(f32[1024,1024]{1,0:T(8,128)} %convolution_bitcast_fusion.p_ref, f32[1024,17]{1,0:T(8,128)} %bitcast.78), custom_call_target="tpu_custom_call" | custom-call | tf_op jit(solution)/shard_map/pallas_call | solution.py:193
  166.5 11.7 %shard_map.38.x_ref = f32[128,256]{1,0:T(8,128)} custom-call(f32[1024,1024]{1,0:T(8,128)} %bitcast.76, f32[1024,1024]{1,0:T(8,128)} %shard_map.37.s_ref), custom_call_target="tpu_custom_call" | custom-call | tf_op jit(solution)/shard_map/pallas_call | solution.py:233
  178.2 7.8 %shard_map.39 = f32[128,64]{1,0:T(8,128)} custom-call(f32[128,256]{1,0:T(8,128)} %shard_map.38.x_ref), custom_call_target="tpu_custom_call" | custom-call | tf_op jit(solution)/shard_map/pallas_call | solution.py:275
  186.0 1.5 copy.87
  (20 shorter events, 16.2 us)
Async XLA Ops:
  53.8 13.2 %copy-start = (f32[17,1024]{1,0:T(8,128)S(1)}, f32[17,1024]{1,0:T(8,128)}, u32[]{:S(2)}) copy-start(f32[17,1024]{1,0:T(8,128)} %param.5) | copy-start | bytes 208900

commit v2 on v1

--- a/solution.py
+++ b/solution.py
@@ -10,14 +10,6 @@
 MESH = pl.DeviceIdType.MESH
 VMEM_LIMIT = 56 * 1024 * 1024
 HOP = 2
-
-
-def hankel(signals, lag_count):
-    steps_count = signals.shape[2]
-    padded = jnp.pad(signals, ((0, 0), (0, 0), (0, lag_count)))
-    return jnp.stack(
-        [padded[:, :, offset : offset + steps_count] for offset in range(lag_count)], axis=1
-    )
 
 
 def greet(axis, peers):
@@ -202,6 +194,98 @@
     )(partial, taps)
 
 
+def gather_kernel(n, x_ref, out_ref, landed, send_sem, recv_sem):
+    me = lax.axis_index("unk")
+    width = x_ref.shape[1]
+    greet("unk", [lax.rem(me + k, n) for k in range(1, n)])
+
+    def copy(k):
+        peer = lax.rem(me + k, n)
+        return pltpu.make_async_remote_copy(
+            src_ref=x_ref, dst_ref=landed.at[me],
+            send_sem=send_sem.at[k], recv_sem=recv_sem.at[k],
+            device_id={"unk": peer}, device_id_type=MESH)
+
+    for k in range(1, n):
+        copy(k).start()
+    landed[me] = x_ref[...]
+    for k in range(1, n):
+        copy(k).wait_recv()
+    for piece in range(n):
+        out_ref[:, piece * width : (piece + 1) * width] = landed[piece]
+    for k in range(1, n):
+        copy(k).wait_send()
+
+
+def gathered(part, n):
+    rows, width = part.shape
+    return pl.pallas_call(
+        functools.partial(gather_kernel, n),
+        out_shape=jax.ShapeDtypeStruct((rows, n * width), jnp.float32),
+        in_specs=[pl.BlockSpec(memory_space=pltpu.VMEM)],
+        out_specs=pl.BlockSpec(memory_space=pltpu.VMEM),
+        scratch_shapes=[
+            pltpu.VMEM((n, rows, width), jnp.float32),
+            pltpu.SemaphoreType.DMA((n,)),
+            pltpu.SemaphoreType.DMA((n,)),
+        ],
+        compiler_params=pltpu.CompilerParams(
+            collective_id=2, has_side_effects=True, vmem_limit_bytes=VMEM_LIMIT
+        ),
+    )(part)
+
+
+def adjoint_kernel(lag_count, vectors, sig_ref, k_ref, out_ref, high, low):
+    steps_count = sig_ref.shape[1]
+
+    @pl.when(pl.program_id(0) == 0)
+    def _():
+        time = lax.broadcasted_iota(jnp.int32, (lag_count, steps_count), 1)
+        lag = lax.broadcasted_iota(jnp.int32, (lag_count, steps_count), 0)
+
+        @pl.loop(0, sig_ref.shape[0] // vectors)
+        def _(sensor):
+            rows = pl.ds(pl.multiple_of(sensor * lag_count, lag_count), lag_count)
+            for vector in range(vectors):
+                series = sig_ref[pl.ds(sensor * vectors + vector, 1), :]
+                moved = jnp.broadcast_to(series, (lag_count, steps_count))
+                bit = 1
+                while bit < lag_count:
+                    moved = jnp.where(
+                        (lag & bit) != 0, pltpu.roll(moved, steps_count - bit, 1), moved
+                    )
+                    bit *= 2
+                columns = slice(vector * steps_count, (vector + 1) * steps_count)
+                moved = jnp.where(time + lag < steps_count, moved, 0.0)
+                high[rows, columns], low[rows, columns] = split(moved)
+
+    k_high, k_low = split(k_ref[...].T)
+    dot = functools.partial(jnp.dot, preferred_element_type=jnp.float32)
+    for vector in range(vectors):
+        columns = slice(vector * steps_count, (vector + 1) * steps_count)
+        out_ref[:, columns] = dot(k_high, high[:, columns]) + (
+            dot(k_high, low[:, columns]) + dot(k_low, high[:, columns])
+        )
+
+
+def adjoint(series, kernel, lag_count, vectors):
+    rows, unk_dev = kernel.shape
+    steps_count = series.shape[1]
+    tile = min(256, unk_dev)
+    return pl.pallas_call(
+        functools.partial(adjoint_kernel, lag_count, vectors),
+        grid=(unk_dev // tile,),
+        out_shape=jax.ShapeDtypeStruct((unk_dev, vectors * steps_count), jnp.float32),
+        in_specs=[
+            pl.BlockSpec(series.shape, lambda i: (0, 0)),
+            pl.BlockSpec((rows, tile), lambda i: (0, i)),
+        ],
+        out_specs=pl.BlockSpec((tile, vectors * steps_count), lambda i: (i, 0)),
+        scratch_shapes=[pltpu.VMEM((rows, vectors * steps_count), jnp.bfloat16)] * 2,
+        compiler_params=pltpu.CompilerParams(vmem_limit_bytes=VMEM_LIMIT),
+    )(series, kernel)
+
+
 def forward_kernel(lag_count, vectors, k_ref, s_ref, out_ref, high, low):
     @pl.when(pl.program_id(0) == 0)
     def _():
@@ -290,13 +374,12 @@
 
 
 def on_device(signals, kernel, tap_weights, *, sens_count, unk_count):
-    whole_signals = lax.all_gather(signals, "unk", axis=2, tiled=True)
     sens_rows, lag_count, unk_dev = kernel.shape
-    _, vectors, steps_count = whole_signals.shape
+    _, vectors, width = signals.shape
+    steps_count = width * unk_count
+    series = gathered(signals.reshape(sens_rows * vectors, width), unk_count)
     flat_kernel = kernel.reshape(sens_rows * lag_count, unk_dev)
-    window = hankel(whole_signals, lag_count)
-    window = window.reshape(sens_rows * lag_count, vectors * steps_count)
-    partial = jnp.einsum("ku,kt->ut", flat_kernel, window, precision=lax.Precision.HIGH)
+    partial = adjoint(series, flat_kernel, lag_count, vectors)
     smoothed = summed_smoothed(partial, tap_weights.T, steps_count, sens_count)
     product = forward(flat_kernel, smoothed, lag_count, vectors)
     return scattered(product, unk_count).reshape(signals.shape)

time: 188 us -> 152 us (0.81)
  local copies, waits for them, and re-layouts: 51 us -> 3.43 us
  Pallas kernels: 118 us -> 148 us
  matrix products: 9.93 us -> 0 us
  blocking collectives: 8.51 us -> 0 us
    unnamed x37 -> x2, local copies, waits for them, and re-layouts: 35.1 us -> 3.43 us
    pallas_call x0 -> x2, Pallas kernels: none -> 29.8 us  [the longest x1 21.6 us: adjoint(): pl.pallas_call(functools.partial(adjoint_kernel, lag_count, vectors), gri...]
    another operation x2 -> x0, local copies, waits for them, and re-layouts: 15.9 us -> none  [hankel(): jnp.stack([padded[:, :, offset:offset + steps_count] for offset in range(...]
    dot_general x1 -> x0, matrix products: 9.93 us -> none  [on_device(): jnp.einsum('ku,kt->ut', flat_kernel, window, precision=lax.Precision.HIGH)]
    all_gather x1 -> x0, blocking collectives: 8.51 us -> none  [on_device(): whole_signals = lax.all_gather(signals, 'unk', axis=2, tiled=True)]
where the time goes in v2:
time: 152 us; the launch traced here: 151 us
  Pallas kernels  148 us (97%)
  local copies, waits for them, and re-layouts  3.43 us (2%)
    pallas_call x1, Pallas kernels, summed_smoothed(): pl.pallas_call(functools.partial(sum_kernel, sens_count // 2, chunks, ste...  99 us
    pallas_call x1, Pallas kernels, adjoint(): pl.pallas_call(functools.partial(adjoint_kernel, lag_count, vectors), gri...  21.6 us
    pallas_call x1, Pallas kernels, forward(): pl.pallas_call(functools.partial(forward_kernel, lag_count, vectors), gri...  11.7 us
    pallas_call x1, Pallas kernels, gathered(): pl.pallas_call(functools.partial(gather_kernel, n), out_shape=jax.ShapeDt...  8.13 us
    pallas_call x1, Pallas kernels, scattered(): pl.pallas_call(functools.partial(scatter_kernel, n), out_shape=jax.ShapeD...  7.46 us
    unnamed x2, local copies, waits for them, and re-layouts  3.43 us

profile of v2, /device:TPU:1, one launch (start us, length us, event | category | flops | bytes accessed | tf_op | source)
XLA Modules:
  0.0 151.4 jit_solution(568056648386181348)
XLA Ops:
  0.0 8.1 %shard_map.37.sig_ref = f32[128,256]{1,0:T(8,128)} custom-call(f32[128,64]{1,0:T(8,128)} %bitcast.8), custom_call_target="tpu_custom_call" | custom-call | tf_op jit(solution)/shard_map/pallas_call | solution.py:222
  8.1 2.0 %copy.4 = f32[17,1024]{0,1:T(8,128)} copy(f32[17,1024]{1,0:T(8,128)} %param.5) | data formatting | bytes 139264 | tf_op args[2]
  10.1 21.6 %shard_map.38.p_ref = f32[1024,1024]{1,0:T(8,128)} custom-call(f32[128,256]{1,0:T(8,128)} %shard_map.37.sig_ref, f32[1024,1024]{1,0:T(8,128)} %bitcast.4), custom_call_target="tpu_custom_call" | custom-call | tf_op jit(solution)/shard_map/pallas_call | solution.py:275
  31.7 99.0 %shard_map.39.s_ref = f32[1024,1024]{1,0:T(8,128)} custom-call(f32[1024,1024]{1,0:T(8,128)} %shard_map.38.p_ref, f32[1024,17]{1,0:T(8,128)} %bitcast.6), custom_call_target="tpu_custom_call" | custom-call | tf_op jit(solution)/shard_map/pallas_call | solution.py:185
  130.8 11.7 %shard_map.40.x_ref = f32[128,256]{1,0:T(8,128)} custom-call(f32[1024,1024]{1,0:T(8,128)} %bitcast.5, f32[1024,1024]{1,0:T(8,128)} %shard_map.39.s_ref), custom_call_target="tpu_custom_call" | custom-call | tf_op jit(solution)/shard_map/pallas_call | solution.py:317
  142.5 7.5 %shard_map.41 = f32[128,64]{1,0:T(8,128)} custom-call(f32[128,256]{1,0:T(8,128)} %shard_map.40.x_ref), custom_call_target="tpu_custom_call" | custom-call | tf_op jit(solution)/shard_map/pallas_call | solution.py:359
  150.0 1.5 copy.6

commit v3 on v2

--- a/solution.py
+++ b/solution.py
@@ -43,8 +43,41 @@
     return jnp.concatenate(pieces, axis=1)
 
 
-def sum_kernel(chain, chunks, steps_count, p_ref, tap_ref, out_ref, y_in, own, up_in, up_out,
-               down_in, down_out, sems):
+def build_window(lag_count, vectors, sig_ref, high, low):
+    steps_count = sig_ref.shape[1]
+    time = lax.broadcasted_iota(jnp.int32, (lag_count, steps_count), 1)
+    lag = lax.broadcasted_iota(jnp.int32, (lag_count, steps_count), 0)
+
+    @pl.loop(0, sig_ref.shape[0] // vectors)
+    def _(sensor):
+        rows = pl.ds(pl.multiple_of(sensor * lag_count, lag_count), lag_count)
+        for vector in range(vectors):
+            series = sig_ref[pl.ds(sensor * vectors + vector, 1), :]
+            moved = jnp.broadcast_to(series, (lag_count, steps_count))
+            bit = 1
+            while bit < lag_count:
+                moved = jnp.where(
+                    (lag & bit) != 0, pltpu.roll(moved, steps_count - bit, 1), moved
+                )
+                bit *= 2
+            columns = slice(vector * steps_count, (vector + 1) * steps_count)
+            moved = jnp.where(time + lag < steps_count, moved, 0.0)
+            high[rows, columns], low[rows, columns] = split(moved)
+
+
+def adjoint_tile(kernel_tile, steps_count, high, low, p_ref, rows):
+    k_high, k_low = split(kernel_tile.T)
+    dot = functools.partial(jnp.dot, preferred_element_type=jnp.float32)
+    for first in range(0, high.shape[1], steps_count):
+        columns = slice(first, first + steps_count)
+        p_ref[rows, columns] = dot(k_high, high[:, columns]) + (
+            dot(k_high, low[:, columns]) + dot(k_low, high[:, columns])
+        )
+
+
+def sum_kernel(chain, chunks, lag_count, vectors, tile, sig_ref, k_ref, tap_ref, out_ref, y_in,
+               own, up_in, up_out, down_in, down_out, p_ref, high, low, sems):
+    steps_count = sig_ref.shape[1]
     n = 2 * chain
     me = lax.axis_index("sens")
     z, y = me // 2, me % 2
@@ -105,9 +138,21 @@
 
     pl.semaphore_wait(barrier, 1 + jnp.where(not_last, 1, 0) + jnp.where(not_first, 1, 0))
 
-    @pl.loop(0, chunks)
-    def _(c):
-        y_copy(c).start()
+    build_window(lag_count, vectors, sig_ref, high, low)
+
+    @pl.loop(0, half_rows // tile)
+    def _(part):
+        place = pl.ds(pl.multiple_of((1 - y) * half_rows + part * tile, tile), tile)
+        adjoint_tile(k_ref[:, place], steps_count, high, low, p_ref, place)
+
+        @pl.loop(0, tile // rows)
+        def _(c):
+            y_copy(part * (tile // rows) + c).start()
+
+    @pl.loop(0, half_rows // tile)
+    def _(part):
+        place = pl.ds(pl.multiple_of(y * half_rows + part * tile, tile), tile)
+        adjoint_tile(k_ref[:, place], steps_count, high, low, p_ref, place)
 
     lag_up, lag_down = HOP * z, HOP * (chain - 1 - z)
     lag_last = HOP * (chain - 1)
@@ -178,20 +223,25 @@
             down_copy(c).wait_send()
 
 
-def summed_smoothed(partial, taps, steps_count, sens_count):
-    unk_dev, columns = partial.shape
+def summed_smoothed(series, kernel, taps, lag_count, vectors, sens_count):
+    rows, unk_dev = kernel.shape
+    columns = vectors * series.shape[1]
+    tile = 128
     chunks = max(1, unk_dev // 2 // 32)
     half = pltpu.VMEM((unk_dev // 2, columns), jnp.float32)
     return pl.pallas_call(
-        functools.partial(sum_kernel, sens_count // 2, chunks, steps_count),
-        out_shape=jax.ShapeDtypeStruct(partial.shape, jnp.float32),
-        in_specs=[pl.BlockSpec(memory_space=pltpu.VMEM)] * 2,
+        functools.partial(sum_kernel, sens_count // 2, chunks, lag_count, vectors, tile),
+        out_shape=jax.ShapeDtypeStruct((unk_dev, columns), jnp.float32),
+        in_specs=[pl.BlockSpec(memory_space=pltpu.VMEM)] * 3,
         out_specs=pl.BlockSpec(memory_space=pltpu.VMEM),
-        scratch_shapes=[half] * 6 + [pltpu.SemaphoreType.DMA((8, chunks))],
+        scratch_shapes=[half] * 6
+        + [pltpu.VMEM((unk_dev, columns), jnp.float32)]
+        + [pltpu.VMEM((rows, columns), jnp.bfloat16)] * 2
+        + [pltpu.SemaphoreType.DMA((8, chunks))],
         compiler_params=pltpu.CompilerParams(
             collective_id=0, has_side_effects=True, vmem_limit_bytes=VMEM_LIMIT
         ),
-    )(partial, taps)
+    )(series, kernel, taps)
 
 
 def gather_kernel(n, x_ref, out_ref, landed, send_sem, recv_sem):
@@ -233,57 +283,6 @@
             collective_id=2, has_side_effects=True, vmem_limit_bytes=VMEM_LIMIT
         ),
     )(part)
-
-
-def adjoint_kernel(lag_count, vectors, sig_ref, k_ref, out_ref, high, low):
-    steps_count = sig_ref.shape[1]
-
-    @pl.when(pl.program_id(0) == 0)
-    def _():
-        time = lax.broadcasted_iota(jnp.int32, (lag_count, steps_count), 1)
-        lag = lax.broadcasted_iota(jnp.int32, (lag_count, steps_count), 0)
-
-        @pl.loop(0, sig_ref.shape[0] // vectors)
-        def _(sensor):
-            rows = pl.ds(pl.multiple_of(sensor * lag_count, lag_count), lag_count)
-            for vector in range(vectors):
-                series = sig_ref[pl.ds(sensor * vectors + vector, 1), :]
-                moved = jnp.broadcast_to(series, (lag_count, steps_count))
-                bit = 1
-                while bit < lag_count:
-                    moved = jnp.where(
-                        (lag & bit) != 0, pltpu.roll(moved, steps_count - bit, 1), moved
-                    )
-                    bit *= 2
-                columns = slice(vector * steps_count, (vector + 1) * steps_count)
-                moved = jnp.where(time + lag < steps_count, moved, 0.0)
-                high[rows, columns], low[rows, columns] = split(moved)
-
-    k_high, k_low = split(k_ref[...].T)
-    dot = functools.partial(jnp.dot, preferred_element_type=jnp.float32)
-    for vector in range(vectors):
-        columns = slice(vector * steps_count, (vector + 1) * steps_count)
-        out_ref[:, columns] = dot(k_high, high[:, columns]) + (
-            dot(k_high, low[:, columns]) + dot(k_low, high[:, columns])
-        )
-
-
-def adjoint(series, kernel, lag_count, vectors):
-    rows, unk_dev = kernel.shape
-    steps_count = series.shape[1]
-    tile = min(256, unk_dev)
-    return pl.pallas_call(
-        functools.partial(adjoint_kernel, lag_count, vectors),
-        grid=(unk_dev // tile,),
-        out_shape=jax.ShapeDtypeStruct((unk_dev, vectors * steps_count), jnp.float32),
-        in_specs=[
-            pl.BlockSpec(series.shape, lambda i: (0, 0)),
-            pl.BlockSpec((rows, tile), lambda i: (0, i)),
-        ],
-        out_specs=pl.BlockSpec((tile, vectors * steps_count), lambda i: (i, 0)),
-        scratch_shapes=[pltpu.VMEM((rows, vectors * steps_count), jnp.bfloat16)] * 2,
-        compiler_params=pltpu.CompilerParams(vmem_limit_bytes=VMEM_LIMIT),
-    )(series, kernel)
 
 
 def forward_kernel(lag_count, vectors, k_ref, s_ref, out_ref, high, low):
@@ -376,11 +375,11 @@
 def on_device(signals, kernel, tap_weights, *, sens_count, unk_count):
     sens_rows, lag_count, unk_dev = kernel.shape
     _, vectors, width = signals.shape
-    steps_count = width * unk_count
     series = gathered(signals.reshape(sens_rows * vectors, width), unk_count)
     flat_kernel = kernel.reshape(sens_rows * lag_count, unk_dev)
-    partial = adjoint(series, flat_kernel, lag_count, vectors)
-    smoothed = summed_smoothed(partial, tap_weights.T, steps_count, sens_count)
+    smoothed = summed_smoothed(
+        series, flat_kernel, tap_weights.T, lag_count, vectors, sens_count
+    )
     product = forward(flat_kernel, smoothed, lag_count, vectors)
     return scattered(product, unk_count).reshape(signals.shape)
 

time: 152 us -> 143 us (0.941)
  Pallas kernels: 148 us -> 139 us
    pallas_call x2 -> x1, Pallas kernels: 121 us -> 112 us  [summed_smoothed(): pl.pallas_call(functools.partial(sum_kernel, sens_count // 2, chunks, lag...]
where the time goes in v3:
time: 143 us; the launch traced here: 142 us
  Pallas kernels  139 us (97%)
  local copies, waits for them, and re-layouts  3.38 us (2%)
    pallas_call x1, Pallas kernels, summed_smoothed(): pl.pallas_call(functools.partial(sum_kernel, sens_count // 2, chunks, lag...  112 us
    pallas_call x1, Pallas kernels, forward(): pl.pallas_call(functools.partial(forward_kernel, lag_count, vectors), gri...  11.7 us
    pallas_call x1, Pallas kernels, gathered(): pl.pallas_call(functools.partial(gather_kernel, n), out_shape=jax.ShapeDt...  8.14 us
    pallas_call x1, Pallas kernels, scattered(): pl.pallas_call(functools.partial(scatter_kernel, n), out_shape=jax.ShapeD...  7.48 us
    unnamed x2, local copies, waits for them, and re-layouts  3.38 us

profile of v3, /device:TPU:1, one launch (start us, length us, event | category | flops | bytes accessed | tf_op | source)
XLA Modules:
  0.0 142.5 jit_solution(13989484568189939861)
XLA Ops:
  0.0 8.1 %shard_map.37.sig_ref = f32[128,256]{1,0:T(8,128)} custom-call(f32[128,64]{1,0:T(8,128)} %bitcast.8), custom_call_target="tpu_custom_call" | custom-call | tf_op jit(solution)/shard_map/pallas_call | solution.py:272
  8.1 1.9 %copy.4 = f32[17,1024]{0,1:T(8,128)} copy(f32[17,1024]{1,0:T(8,128)} %param.5) | data formatting | bytes 139264 | tf_op args[2]
  10.1 111.8 %shard_map.38.s_ref = f32[1024,1024]{1,0:T(8,128)} custom-call(f32[128,256]{1,0:T(8,128)} %shard_map.37.sig_ref, f32[1024,1024]{1,0:T(8,128)} %bitcast.4, f32[1024,17]{1,0:T(8,128)} %bitcast.6), custom_call_target="tpu_custom_call" | custom-call | tf_op jit(solution)/shard_map/pallas_call | solution.py:232
  121.8 11.7 %shard_map.39.x_ref = f32[128,256]{1,0:T(8,128)} custom-call(f32[1024,1024]{1,0:T(8,128)} %bitcast.5, f32[1024,1024]{1,0:T(8,128)} %shard_map.38.s_ref), custom_call_target="tpu_custom_call" | custom-call | tf_op jit(solution)/shard_map/pallas_call | solution.py:316
  133.5 7.5 %shard_map.40 = f32[128,64]{1,0:T(8,128)} custom-call(f32[128,256]{1,0:T(8,128)} %shard_map.39.x_ref), custom_call_target="tpu_custom_call" | custom-call | tf_op jit(solution)/shard_map/pallas_call | solution.py:358
  141.0 1.5 %copy.6 = f32[32,4,64]{2,1,0:T(4,128)} copy(f32[32,4,64]{2,1,0:T(4,128)} %bitcast.7) | data formatting | bytes 65536

commit v4 on v3

--- a/solution.py
+++ b/solution.py
@@ -75,8 +75,9 @@
         )
 
 
-def sum_kernel(chain, chunks, lag_count, vectors, tile, sig_ref, k_ref, tap_ref, out_ref, y_in,
-               own, up_in, up_out, down_in, down_out, p_ref, high, low, sems):
+def sum_kernel(chain, chunks, lag_count, vectors, tile, sig_ref, k_ref, tap_ref, data_ref, y_in,
+               own, up_in, up_out, down_in, down_out, p_ref, out_ref, high, low, s_high, s_low,
+               product, sems):
     steps_count = sig_ref.shape[1]
     n = 2 * chain
     me = lax.axis_index("sens")
@@ -208,11 +209,53 @@
             )
             back_copy(last).start()
 
+    def half_product(h):
+        place = pl.ds(pl.multiple_of(h * half_rows, half_rows), half_rows)
+        s_high[...], s_low[...] = split(out_ref[place, :])
+        return place
+
+    def group_product(group_rows, place, columns):
+        k_high, k_low = split(k_ref[group_rows, place])
+        dot = functools.partial(jnp.dot, preferred_element_type=jnp.float32)
+        return dot(k_high, s_high[:, columns]) + (
+            dot(k_high, s_low[:, columns]) + dot(k_low, s_high[:, columns])
+        )
+
+    group = min(8, k_ref.shape[0] // lag_count)
+    group_size = group * lag_count
+    group_count = k_ref.shape[0] // group_size
+    spans = [slice(v * steps_count, (v + 1) * steps_count) for v in range(vectors)]
+    mine = half_product(y)
+
+    @pl.loop(0, group_count)
+    def _(g):
+        group_rows = pl.ds(pl.multiple_of(g * group_size, group_size), group_size)
+        for columns in spans:
+            product[group_rows, columns] = group_product(group_rows, mine, columns)
+
+    @pl.loop(0, chunks)
+    def _(c):
+        back_wait(c)
+
+    other = half_product(1 - y)
+    time = lax.broadcasted_iota(jnp.int32, (lag_count, steps_count), 1)
+    lag = lax.broadcasted_iota(jnp.int32, (lag_count, steps_count), 0)
+
+    @pl.loop(0, group_count)
+    def _(g):
+        group_rows = pl.ds(pl.multiple_of(g * group_size, group_size), group_size)
+        for vector, columns in enumerate(spans):
+            total = product[group_rows, columns] + group_product(group_rows, other, columns)
+            for sensor in range(group):
+                part = total[sensor * lag_count : (sensor + 1) * lag_count]
+                sheared = pltpu.roll(part, 0, 1, stride=1, stride_axis=0)
+                row = jnp.sum(jnp.where(time >= lag, sheared, 0.0), axis=0, keepdims=True)
+                data_ref[pl.ds((g * group + sensor) * vectors + vector, 1), :] = row
+
     @pl.loop(0, chunks)
     def _(c):
         y_copy(c).wait_send()
         back_copy(c).wait_send()
-        back_wait(c)
 
         @pl.when(not_last)
         def _():
@@ -231,12 +274,14 @@
     half = pltpu.VMEM((unk_dev // 2, columns), jnp.float32)
     return pl.pallas_call(
         functools.partial(sum_kernel, sens_count // 2, chunks, lag_count, vectors, tile),
-        out_shape=jax.ShapeDtypeStruct((unk_dev, columns), jnp.float32),
+        out_shape=jax.ShapeDtypeStruct(series.shape, jnp.float32),
         in_specs=[pl.BlockSpec(memory_space=pltpu.VMEM)] * 3,
         out_specs=pl.BlockSpec(memory_space=pltpu.VMEM),
         scratch_shapes=[half] * 6
-        + [pltpu.VMEM((unk_dev, columns), jnp.float32)]
+        + [pltpu.VMEM((unk_dev, columns), jnp.float32)] * 2
         + [pltpu.VMEM((rows, columns), jnp.bfloat16)] * 2
+        + [pltpu.VMEM((unk_dev // 2, columns), jnp.bfloat16)] * 2
+        + [pltpu.VMEM((rows, columns), jnp.float32)]
         + [pltpu.SemaphoreType.DMA((8, chunks))],
         compiler_params=pltpu.CompilerParams(
             collective_id=0, has_side_effects=True, vmem_limit_bytes=VMEM_LIMIT
@@ -283,48 +328,6 @@
             collective_id=2, has_side_effects=True, vmem_limit_bytes=VMEM_LIMIT
         ),
     )(part)
-
-
-def forward_kernel(lag_count, vectors, k_ref, s_ref, out_ref, high, low):
-    @pl.when(pl.program_id(0) == 0)
-    def _():
-        high[...], low[...] = split(s_ref[...])
-
-    k_high, k_low = split(k_ref[...])
-    dot = functools.partial(jnp.dot, preferred_element_type=jnp.float32)
-    steps_count = s_ref.shape[1] // vectors
-    time = lax.broadcasted_iota(jnp.int32, (lag_count, steps_count), 1)
-    lag = lax.broadcasted_iota(jnp.int32, (lag_count, steps_count), 0)
-    for vector in range(vectors):
-        columns = slice(vector * steps_count, (vector + 1) * steps_count)
-        product = dot(k_high, high[:, columns]) + (
-            dot(k_high, low[:, columns]) + dot(k_low, high[:, columns])
-        )
-        for sensor in range(k_ref.shape[0] // lag_count):
-            part = product[sensor * lag_count : (sensor + 1) * lag_count]
-            sheared = pltpu.roll(part, 0, 1, stride=1, stride_axis=0)
-            row = jnp.sum(jnp.where(time >= lag, sheared, 0.0), axis=0, keepdims=True)
-            place = sensor * vectors + vector
-            out_ref[place : place + 1, :] = row
-
-
-def forward(kernel, smoothed, lag_count, vectors):
-    rows, unk_dev = kernel.shape
-    columns = smoothed.shape[1]
-    group = min(8, rows // lag_count)
-    sens_rows = rows // lag_count
-    return pl.pallas_call(
-        functools.partial(forward_kernel, lag_count, vectors),
-        grid=(sens_rows // group,),
-        out_shape=jax.ShapeDtypeStruct((sens_rows * vectors, columns // vectors), jnp.float32),
-        in_specs=[
-            pl.BlockSpec((group * lag_count, unk_dev), lambda i: (i, 0)),
-            pl.BlockSpec((unk_dev, columns), lambda i: (0, 0)),
-        ],
-        out_specs=pl.BlockSpec((group * vectors, columns // vectors), lambda i: (i, 0)),
-        scratch_shapes=[pltpu.VMEM((unk_dev, columns), jnp.bfloat16)] * 2,
-        compiler_params=pltpu.CompilerParams(vmem_limit_bytes=VMEM_LIMIT),
-    )(kernel, smoothed)
 
 
 def scatter_kernel(n, x_ref, out_ref, stage, landed, send_sem, recv_sem):
@@ -377,10 +380,9 @@
     _, vectors, width = signals.shape
     series = gathered(signals.reshape(sens_rows * vectors, width), unk_count)
     flat_kernel = kernel.reshape(sens_rows * lag_count, unk_dev)
-    smoothed = summed_smoothed(
+    product = summed_smoothed(
         series, flat_kernel, tap_weights.T, lag_count, vectors, sens_count
     )
-    product = forward(flat_kernel, smoothed, lag_count, vectors)
     return scattered(product, unk_count).reshape(signals.shape)
 
 

time: 143 us -> 135 us (0.944)
  Pallas kernels: 139 us -> 131 us
    pallas_call x1 -> x0, Pallas kernels: 11.7 us -> none  [forward(): pl.pallas_call(functools.partial(forward_kernel, lag_count, vectors), gri...]
    pallas_call x1, Pallas kernels: 112 us -> 116 us  [summed_smoothed(): pl.pallas_call(functools.partial(sum_kernel, sens_count // 2, chunks, lag...]
where the time goes in v4:
time: 135 us; the launch traced here: 134 us
  Pallas kernels  131 us (97%)
  local copies, waits for them, and re-layouts  3.38 us (3%)
    pallas_call x1, Pallas kernels, summed_smoothed(): pl.pallas_call(functools.partial(sum_kernel, sens_count // 2, chunks, lag...  116 us
    pallas_call x1, Pallas kernels, gathered(): pl.pallas_call(functools.partial(gather_kernel, n), out_shape=jax.ShapeDt...  8.12 us
    pallas_call x1, Pallas kernels, scattered(): pl.pallas_call(functools.partial(scatter_kernel, n), out_shape=jax.ShapeD...  7.45 us
    unnamed x2, local copies, waits for them, and re-layouts  3.38 us

profile of v4, /device:TPU:1, one launch (start us, length us, event | category | flops | bytes accessed | tf_op | source)
XLA Modules:
  0.0 134.5 jit_solution(3540376370630622768)
XLA Ops:
  0.0 8.1 %shard_map.37.sig_ref = f32[128,256]{1,0:T(8,128)} custom-call(f32[128,64]{1,0:T(8,128)} %bitcast.7), custom_call_target="tpu_custom_call" | custom-call | tf_op jit(solution)/shard_map/pallas_call | solution.py:317
  8.1 1.9 %copy.4 = f32[17,1024]{0,1:T(8,128)} copy(f32[17,1024]{1,0:T(8,128)} %param.5) | data formatting | bytes 139264 | tf_op args[2]
  10.0 115.5 %shard_map.38.x_ref = f32[128,256]{1,0:T(8,128)} custom-call(f32[128,256]{1,0:T(8,128)} %shard_map.37.sig_ref, f32[1024,1024]{1,0:T(8,128)} %bitcast.4, f32[1024,17]{1,0:T(8,128)} %bitcast.5), custom_call_target="tpu_custom_call" | custom-call | tf_op jit(solution)/shard_map/pallas_call | solution.py:275
  125.6 7.5 %shard_map.39 = f32[128,64]{1,0:T(8,128)} custom-call(f32[128,256]{1,0:T(8,128)} %shard_map.38.x_ref), custom_call_target="tpu_custom_call" | custom-call | tf_op jit(solution)/shard_map/pallas_call | solution.py:361
  133.0 1.5 %copy.6 = f32[32,4,64]{2,1,0:T(4,128)} copy(f32[32,4,64]{2,1,0:T(4,128)} %bitcast.6) | data formatting | bytes 65536
